TPU v7x, 32 devices: a whole 2x2x4 slice. The times are simulated.
32 devices in a mesh: space: 8 (over z, x), vel: 4 (over y, core).
Axes of the slice: x: 2, y: 2, z: 4, core: 2. Of those that a mesh axis runs over, the one named last changes fastest.
Arguments:
- velocity_dist: bfloat16 [32768, 2048], P('vel', 'space'), may hold values from -6 to 6
- macro_state: float32 [13, 2048], P(None, ('space', 'vel')), may hold values from -2 to 2
- collision_rate: float32 [2048], P('space'), may hold values from 0.25 to 2
- wall_flags: int32 [2048], P('space'), may hold values 0 or 1
- diffusivity: float32 [13], replicated, may hold values from 0.5 to 8
- coupling: float32 [13, 13], replicated, may hold values from -0.25 to 4.5, as said below
Outputs:
- dist_out: bfloat16 [32768, 2048], P('vel', 'space')
- macro_out: float32 [13, 2048], P(None, ('space', 'vel'))
Inputs may be any that keep to these rules, and one draw needn't show every extreme that they name: `coupling`: symmetric, with each diagonal entry larger than the sum of magnitudes of the other entries of its row.
All inputs are finite; a program needn't handle non-finite values. No bound on the sum of `wall_flags` on one device may be relied on, other than what follows from the above.
Results may differ from a plain program's by a relative error of at most 0.001.
Values sent between devices are 32-bit elements; how exact they have to be, the bound alone decides.
A program may use at most 64 MiB of HBM per device.

v0:
```python
import math

import jax
import jax.numpy as jnp
import numpy as np
from jax import lax
from jax.experimental import pallas as pl
from jax.experimental.pallas import tpu as pltpu
from jax.sharding import PartitionSpec as P

NV1 = 32
ITERS = 3
SWEEPS = 2
K = 13
Q = 8
HALO = 8
TILE = 128
MESH = pl.DeviceIdType.MESH

speed_limit = 4.0
time_step = 0.125
shakhov_weights = (1.0,) * 5 + (0.0,) * 5 + (1.0 / 3.0,) * 3


def two_parts(x):
    high = np.asarray(x, np.float32).astype(jnp.bfloat16)
    low = (np.asarray(x, np.float32) - high.astype(np.float32)).astype(jnp.bfloat16)
    return high, low


def tables():
    spacing = 2.0 * speed_limit / NV1
    v = (np.arange(NV1) + 0.5) * spacing - speed_limit
    w1 = np.exp(-0.5 * v * v) * spacing / math.sqrt(2.0 * math.pi)
    y = np.repeat(v, NV1)
    z = np.tile(v, NV1)
    w_yz = np.repeat(w1, NV1) * np.tile(w1, NV1)
    phi = np.stack([np.ones_like(y), y, z, y * y, z * z, y * z, y * (y * y + z * z), z * (y * y + z * z)])
    beta = np.zeros((NV1, Q, 16))
    r6, r12, r10 = math.sqrt(6.0), math.sqrt(12.0), math.sqrt(10.0)
    beta[:, 0, 0] = 1.0
    beta[:, 0, 1] = v
    beta[:, 1, 2] = 1.0
    beta[:, 2, 3] = 1.0
    beta[:, 0, 4], beta[:, 3, 4], beta[:, 4, 4] = (v * v - 3.0) / r6, 1.0 / r6, 1.0 / r6
    beta[:, 1, 5] = v
    beta[:, 2, 6] = v
    beta[:, 5, 7] = 1.0
    beta[:, 0, 8], beta[:, 3, 8] = 0.5 * v * v, -0.5
    beta[:, 0, 9], beta[:, 3, 9], beta[:, 4, 9] = v * v / r12, 1.0 / r12, -2.0 / r12
    beta[:, 0, 10], beta[:, 3, 10], beta[:, 4, 10] = v * (v * v - 5.0) / r10, v / r10, v / r10
    beta[:, 1, 11], beta[:, 6, 11] = (v * v - 5.0) / r10, 1.0 / r10
    beta[:, 2, 12], beta[:, 7, 12] = (v * v - 5.0) / r10, 1.0 / r10
    gram = (phi * w_yz) @ phi.T
    rows = NV1 * Q
    project = np.einsum("qr,vrk->vqk", gram, beta).reshape(rows, 16)
    moments = (w1[:, None, None] * beta).reshape(rows, 16).T
    inner = moments @ project

    def left(a):
        high, low = two_parts(a)
        return np.concatenate([high, high, low], axis=1)

    reduce_h, reduce_l = two_parts(phi * w_yz)
    phi_h, phi_l = two_parts(phi)
    m_h, m_l = two_parts(moments)
    return dict(
        reduce=np.concatenate([reduce_h, reduce_l]),
        phi=np.concatenate([phi_h, phi_h, phi_l, phi_l]),
        project=left(project),
        beta=left(beta.reshape(rows, 16)),
        moments=np.concatenate([m_h, m_l]),
        inner=left(inner),
    )


def split(x):
    high = x.astype(jnp.bfloat16)
    return high, (x - high.astype(jnp.float32)).astype(jnp.bfloat16)


def dot(a, b):
    return jnp.dot(a, b, preferred_element_type=jnp.float32)


def dot_parts(left, x):
    high, low = split(x)
    return dot(left, jnp.concatenate([high, low, high], axis=0))


def roll(x, shift):
    return pltpu.roll(x, shift % x.shape[1], 1)


def moments_kernel(
    S, N,
    h_ref, macro_ref, rate_ref, wall_ref, diff_ref, coup_ref,
    reduce_ref, project_ref, beta_ref, moments_ref, inner_ref,
    zc_ref, coef_ref, halo_ref, out_ref,
    h_buf, g_all, cur_stage, cur_peers, cur_left, cur_right,
    pack_l, pack_r, from_left, from_right, edge_send, edge_recv, sums, coup_pad,
    h_sem, g_ssem, g_rsem, c_ssem, c_rsem, cl_ssem, cl_rsem, cr_ssem, cr_rsem,
    pl_ssem, pl_rsem, pr_ssem, pr_rsem, e_ssem, e_rsem, s_ssem, s_rsem,
):
    L = h_ref.shape[1]
    W = L + TILE
    width = macro_ref.shape[1]
    per_tile = TILE // width
    plane = NV1 * NV1
    nvx = h_ref.shape[0] // plane
    R = nvx * Q
    group = edge_send.shape[0]
    members = nvx // group
    s = lax.axis_index("space")
    p = lax.axis_index("vel")
    positive = p >= N // 2
    has_left = s > 0
    has_right = s < S - 1
    f32 = jnp.float32

    for j in range(nvx):
        pltpu.make_async_copy(h_ref.at[pl.ds(j * plane, plane)], h_buf.at[pl.ds(j * plane, plane)], h_sem.at[j]).start()

    cur_left[...] = jnp.zeros_like(cur_left)
    cur_right[...] = jnp.zeros_like(cur_right)
    from_left[...] = jnp.zeros_like(from_left)
    from_right[...] = jnp.zeros_like(from_right)
    edge_recv[...] = jnp.zeros_like(edge_recv)

    barrier = pltpu.get_barrier_semaphore()

    def greet(device):
        pl.semaphore_signal(barrier, inc=1, device_id=device, device_id_type=MESH)

    for k in range(1, N):
        greet((s, lax.rem(p + k, N)))

    @pl.when(has_left)
    def _():
        for q in range(N):
            greet((s - 1, q))

    @pl.when(has_right)
    def _():
        for q in range(N):
            greet((s + 1, q))

    for t in range(S):
        @pl.when((t != s) & (t != s - 1) & (t != s + 1))
        def _():
            greet((t, p))

    beside = has_left.astype(jnp.int32) + has_right.astype(jnp.int32)
    greetings = (N - 1) + N * beside + (S - 1 - beside)

    relax = time_step * rate_ref[...] * (1.0 + wall_ref[...].astype(f32))
    edge_relax = jnp.where(p == 0, relax[:, :TILE], relax[:, L - TILE:])
    cur_stage[...] = jnp.zeros_like(cur_stage)
    cur_stage[0:K, :] = jnp.concatenate([macro_ref[...]] * per_tile, axis=1)
    cur_stage[K:K + 1, :] = edge_relax
    cur_peers[p] = cur_stage[...]
    coup_pad[...] = jnp.zeros_like(coup_pad)
    coup_pad[0:K, 0:K] = coup_ref[...]

    row8 = lax.broadcasted_iota(jnp.int32, (8, L), 0)
    col8 = lax.broadcasted_iota(jnp.int32, (8, L), 1)
    upwind_cell = jnp.where(positive, L - 1 - col8, col8)
    pick = []
    for m in range(members):
        t = row8 - 4 * m
        pick.append(((t == upwind_cell) & (t >= 0) & (t < ITERS)).astype(f32).astype(jnp.bfloat16))

    reduce = reduce_ref[...]
    lane8 = lax.broadcasted_iota(jnp.int32, (8, TILE), 1)
    packed_l = jnp.zeros((8, TILE), f32)
    packed_r = jnp.zeros((8, TILE), f32)

    def cur_copy(dst, ssem, rsem, device):
        return pltpu.make_async_remote_copy(
            src_ref=cur_stage, dst_ref=dst, send_sem=ssem, recv_sem=rsem, device_id=device, device_id_type=MESH)

    def g_copy(g, k):
        rows = pl.ds(pl.multiple_of(p * R + g * members * Q, 8), members * Q)
        return pltpu.make_async_remote_copy(
            src_ref=g_all.at[rows, pl.ds(0, L)], dst_ref=g_all.at[rows, pl.ds(0, L)],
            send_sem=g_ssem.at[g, k], recv_sem=g_rsem.at[g, p],
            device_id=(s, lax.rem(p + k, N)), device_id_type=MESH)

    def edge_copy(g, target):
        return pltpu.make_async_remote_copy(
            src_ref=edge_send.at[g], dst_ref=edge_recv.at[g],
            send_sem=e_ssem.at[g], recv_sem=e_rsem.at[g],
            device_id=(target, p), device_id_type=MESH)

    downwind = jnp.where(positive, s + 1, s - 1)
    has_down = (downwind >= 0) & (downwind < S)
    has_up = jnp.where(positive, s - 1, S - 2 - s) >= 0

    for g in range(group):
        edge = jnp.zeros((8, plane), f32)
        for m in range(members):
            j = g * members + m
            pltpu.make_async_copy(
                h_ref.at[pl.ds(j * plane, plane)], h_buf.at[pl.ds(j * plane, plane)], h_sem.at[j]).wait()
            block = h_buf[j * plane:(j + 1) * plane, :]
            both = dot(reduce, block)
            value = both[:Q] + both[Q:]
            g_all[pl.ds(pl.multiple_of(p * R + j * Q, 8), Q), 0:L] = value
            edge = edge + lax.dot_general(pick[m], block, (((1,), (1,)), ((), ())), preferred_element_type=f32)
            here = (lane8 >= HALO * j) & (lane8 < HALO * (j + 1))
            packed_l = jnp.where(here, roll(value[:, :TILE], HALO * j), packed_l)
            packed_r = jnp.where(here, roll(value[:, L - TILE:], HALO * j - (TILE - HALO)), packed_r)
        edge_send[g] = edge
        if g == 0:
            pl.semaphore_wait(barrier, greetings)
            for k in range(1, N):
                cur_copy(cur_peers.at[p], c_ssem.at[k], c_rsem.at[p], (s, lax.rem(p + k, N))).start()

            @pl.when((p == 0) & has_left)
            def _():
                for q in range(N):
                    cur_copy(cur_right, cr_ssem.at[q], cr_rsem, (s - 1, q)).start()

            @pl.when((p == N - 1) & has_right)
            def _():
                for q in range(N):
                    cur_copy(cur_left, cl_ssem.at[q], cl_rsem, (s + 1, q)).start()

        for k in range(1, N):
            g_copy(g, k).start()

        @pl.when(has_down)
        def _():
            edge_copy(g, downwind).start()

    pack_l[...] = packed_l
    pack_r[...] = packed_r

    def pack_copy(src, dst, ssem, rsem, device):
        return pltpu.make_async_remote_copy(
            src_ref=src, dst_ref=dst.at[p], send_sem=ssem, recv_sem=rsem.at[p], device_id=device, device_id_type=MESH)

    @pl.when(has_left)
    def _():
        for q in range(N):
            pack_copy(pack_l, from_right, pl_ssem.at[q], pl_rsem, (s - 1, q)).start()

    @pl.when(has_right)
    def _():
        for q in range(N):
            pack_copy(pack_r, from_left, pr_ssem.at[q], pr_rsem, (s + 1, q)).start()

    vx_row = lax.broadcasted_iota(jnp.int32, (NV1 * Q, 1), 0) // Q
    c_all = time_step * jnp.abs((vx_row.astype(f32) + 0.5) * (2.0 * speed_limit / NV1) - speed_limit)
    own_row = lax.broadcasted_iota(jnp.int32, (R, 1), 0) // Q + p * nvx
    c_own = time_step * jnp.abs((own_row.astype(f32) + 0.5) * (2.0 * speed_limit / NV1) - speed_limit)
    own_vx = lax.broadcasted_iota(jnp.int32, (nvx, 1), 0) + p * nvx
    c_vx = time_step * jnp.abs((own_vx.astype(f32) + 0.5) * (2.0 * speed_limit / NV1) - speed_limit)
    row16 = lax.broadcasted_iota(jnp.int32, (16, 1), 0)
    diffusion = jnp.zeros((16, 1), f32)
    scale = jnp.zeros((16, 1), f32)
    for k in range(K):
        diffusion = jnp.where(row16 == k, diff_ref[k], diffusion)
        scale = jnp.where(row16 == k, shakhov_weights[k], scale)
    lane = lax.broadcasted_iota(jnp.int32, (1, W), 1)
    cell = jnp.where(lane < L + TILE // 2, lane, lane - W) + s * L
    inside = (cell >= 0) & (cell < S * L)
    lane_t = lax.broadcasted_iota(jnp.int32, (1, TILE), 1)
    coupling = coup_pad[...]

    for k in range(1, N):
        q = lax.rem(p + k, N)
        pltpu.make_async_remote_copy(
            src_ref=cur_stage, dst_ref=cur_peers.at[q], send_sem=c_ssem.at[k], recv_sem=c_rsem.at[q],
            device_id=(s, q), device_id_type=MESH).wait_recv()

    @pl.when(has_right)
    def _():
        cur_copy(cur_right, cr_ssem.at[0], cr_rsem, (s, p)).wait_recv()

    @pl.when(has_left)
    def _():
        cur_copy(cur_left, cl_ssem.at[0], cl_rsem, (s, p)).wait_recv()

    tiles = []
    for tile in range(L // TILE):
        value = cur_peers[tile * per_tile]
        for b in range(1, per_tile):
            value = jnp.where(lane_t < b * width, value, cur_peers[tile * per_tile + b])
        tiles.append(value)
    beyond = jnp.where(lane_t < TILE // 2, cur_right[...], cur_left[...])
    current = jnp.concatenate(tiles + [beyond], axis=1)
    current = jnp.where(row16 < K, current, 0.0)
    relax = jnp.concatenate([relax, beyond[K:K + 1]], axis=1)

    def own_shift(x):
        return jnp.where(positive, roll(x, 1), roll(x, -1))

    alpha = 1.0 - c_vx - relax
    weights = [jnp.ones((nvx, W), f32)] + [jnp.zeros((nvx, W), f32)] * ITERS
    for n in range(ITERS):
        shifted = [own_shift(a) for a in weights[:-1]]
        weights = [alpha * weights[0]] + [
            alpha * weights[i] + c_vx * shifted[i - 1] for i in range(1, ITERS + 1)]
    for i in range(ITERS + 1):
        coef_ref[i] = weights[i][:, :L]
    for j in range(nvx):
        m = j % members
        t = row8 - 4 * m
        value = jnp.zeros((8, L), f32)
        for i in range(1, ITERS + 1):
            near = jnp.where(positive, col8, L - 1 - col8)
            value = jnp.where((near + 1 + t == i) & (t >= 0) & (t < ITERS), weights[i][j:j + 1, :L], value)
        high, low = split(value)
        zc_ref[j, 32:48, :] = jnp.concatenate([high.astype(f32), low.astype(f32)], axis=0).astype(jnp.bfloat16)

    for g in range(group):
        for k in range(1, N):
            q = lax.rem(p + k, N)
            rows = pl.ds(pl.multiple_of(q * R + g * members * Q, 8), members * Q)
            pltpu.make_async_remote_copy(
                src_ref=g_all.at[rows, pl.ds(0, L)], dst_ref=g_all.at[rows, pl.ds(0, L)],
                send_sem=g_ssem.at[g, k], recv_sem=g_rsem.at[g, q],
                device_id=(s, q), device_id_type=MESH).wait_recv()

    def pack_wait(dst, ssem, rsem):
        for q in range(N):
            pltpu.make_async_remote_copy(
                src_ref=pack_l, dst_ref=dst.at[q], send_sem=ssem.at[q], recv_sem=rsem.at[q],
                device_id=(s, q), device_id_type=MESH).wait_recv()

    @pl.when(has_right)
    def _():
        pack_wait(from_right, pl_ssem, pl_rsem)

    @pl.when(has_left)
    def _():
        pack_wait(from_left, pr_ssem, pr_rsem)

    for q in range(N):
        right = from_right[q]
        left = from_left[q]
        for j in range(nvx):
            value = jnp.where(lane8 < TILE // 2, roll(right, -HALO * j), roll(left, TILE - HALO - HALO * j))
            g_all[q * R + j * Q:q * R + (j + 1) * Q, L:W] = value

    half = NV1 * Q // 2

    def all_shift(x):
        return jnp.concatenate([roll(x[:half], -1), roll(x[half:], 1)], axis=0)

    def operator(r):
        applied = jnp.dot(coupling, r, precision=lax.Precision.HIGHEST, preferred_element_type=f32)
        applied = applied + diffusion * (2.0 * r - roll(r, 1) - roll(r, -1))
        return jnp.where(inside, applied, 0.0)

    def own_sum(x):
        total = x[:, 0:TILE]
        for tile in range(1, L // TILE):
            total = total + x[:, tile * TILE:(tile + 1) * TILE]
        return jnp.sum(total, axis=0, keepdims=True)

    keep_all = 1.0 - c_all - relax
    keep_own = 1.0 - c_own - relax
    beta_own = beta_ref[pl.ds(pl.multiple_of(p * R, 16), R), :]
    state = g_all[...]
    source = None

    def sum_copy(n, t):
        target = lax.rem(s + t, S)
        return pltpu.make_async_remote_copy(
            src_ref=sums.at[n, s], dst_ref=sums.at[n, s], send_sem=s_ssem.at[n, t], recv_sem=s_rsem.at[n, s],
            device_id=(target, p), device_id_type=MESH)

    for n in range(ITERS):
        moved = keep_all * state + c_all * all_shift(state)
        pull = scale * relax * current
        high, low = split(moved)
        twice = dot(moments_ref[...], high)
        shares = twice[:16] + twice[16:] + dot(moments_ref[0:16, :], low) + dot_parts(inner_ref[...], pull)
        shares = jnp.where(inside, shares, 0.0)
        r = shares - current
        a1 = operator(r)
        a2 = operator(a1)
        sums[n, s] = jnp.concatenate(
            [own_sum(r * r), own_sum(r * a1), own_sum(a1 * a1), own_sum(a1 * a2), jnp.zeros((4, TILE), f32)], axis=0)
        for t in range(1, S):
            sum_copy(n, t).start()
        for t in range(1, S):
            q = lax.rem(s + t, S)
            pltpu.make_async_remote_copy(
                src_ref=sums.at[n, q], dst_ref=sums.at[n, q], send_sem=s_ssem.at[n, t], recv_sem=s_rsem.at[n, q],
                device_id=(q, p), device_id_type=MESH).wait_recv()
        total = sums[n, 0]
        for t in range(1, S):
            total = total + sums[n, t]
        total = jnp.sum(total, axis=1, keepdims=True)
        m0, m1, m2, m3 = (total[i:i + 1] for i in range(4))
        first = m0 / m1
        second = (m0 - 2.0 * first * m1 + first * first * m2) / (m1 - 2.0 * first * m2 + first * first * m3)
        correction = first * r + second * (r - first * a1)
        current = shares + correction
        z = pull + correction
        if n < ITERS - 1:
            state = moved + dot_parts(project_ref[...], z)
        fresh = dot_parts(beta_own, z)
        source = fresh if source is None else keep_own * source + c_own * own_shift(source) + fresh

    for j in range(nvx):
        high, low = split(source[j * Q:(j + 1) * Q, :L])
        pair = jnp.concatenate([high.astype(f32), low.astype(f32)], axis=0).astype(jnp.bfloat16)
        zc_ref[j, 0:16, :] = pair
        zc_ref[j, 16:32, :] = pair

    chosen = current[:, 0:TILE]
    for tile in range(1, L // TILE):
        chosen = jnp.where(p >= tile * per_tile, current[:, tile * TILE:(tile + 1) * TILE], chosen)
    place = lax.rem(p, per_tile)
    for b in range(per_tile):
        @pl.when(place == b)
        def _():
            out_ref[...] = chosen[:K, b * width:(b + 1) * width]

    @pl.when(has_up)
    def _():
        for g in range(group):
            edge_copy(g, s).wait_recv()

    halo_ref[...] = edge_recv[...]

    for k in range(1, N):
        cur_copy(cur_peers.at[p], c_ssem.at[k], c_rsem.at[p], (s, lax.rem(p + k, N))).wait_send()
        for g in range(group):
            g_copy(g, k).wait_send()

    @pl.when((p == 0) & has_left)
    def _():
        for q in range(N):
            cur_copy(cur_right, cr_ssem.at[q], cr_rsem, (s - 1, q)).wait_send()

    @pl.when((p == N - 1) & has_right)
    def _():
        for q in range(N):
            cur_copy(cur_left, cl_ssem.at[q], cl_rsem, (s + 1, q)).wait_send()

    @pl.when(has_down)
    def _():
        for g in range(group):
            edge_copy(g, downwind).wait_send()

    @pl.when(has_left)
    def _():
        for q in range(N):
            pack_copy(pack_l, from_right, pl_ssem.at[q], pl_rsem, (s - 1, q)).wait_send()

    @pl.when(has_right)
    def _():
        for q in range(N):
            pack_copy(pack_r, from_left, pr_ssem.at[q], pr_rsem, (s + 1, q)).wait_send()

    for n in range(ITERS):
        for t in range(1, S):
            sum_copy(n, t).wait_send()


def result_kernel(N, members, h_ref, zc_ref, coef_ref, halo_ref, phi_ref, out_ref):
    j = pl.program_id(0)
    L = h_ref.shape[1]
    positive = lax.axis_index("vel") >= N // 2
    row = lax.broadcasted_iota(jnp.int32, (L, L), 0)
    col = lax.broadcasted_iota(jnp.int32, (L, L), 1)
    distance = jnp.where(positive, col - row, row - col)
    band = jnp.zeros((L, L), jnp.float32)
    for i in range(ITERS + 1):
        band = jnp.where(distance == i, coef_ref[i, pl.ds(j, 1), :], band)
    high, low = split(band)
    block = h_ref[...]
    edge = halo_ref[j // members]
    rows = jnp.concatenate([phi_ref[...], jnp.concatenate([edge, edge], axis=0).astype(jnp.bfloat16)], axis=0)
    total = dot(block, high) + dot(block, low)
    total = total + lax.dot_general(
        rows, zc_ref[0], (((0,), (0,)), ((), ())), preferred_element_type=jnp.float32)
    out_ref[...] = total.astype(jnp.bfloat16)


def solution(mesh):
    S, N = mesh.shape["space"], mesh.shape["vel"]
    table = tables()
    plane = NV1 * NV1

    def per_device(velocity_dist, macro_state, collision_rate, wall_flags, diffusivity, coupling):
        V, L = velocity_dist.shape
        width = macro_state.shape[1]
        nvx = V // plane
        members = 2
        group = nvx // members
        assert N % 2 == 0 and nvx % 2 == 0 and HALO * nvx <= TILE and width >= HALO and TILE % width == 0
        f32, bf16 = jnp.float32, jnp.bfloat16
        vmem = pl.BlockSpec(memory_space=pltpu.VMEM)
        smem = pl.BlockSpec(memory_space=pltpu.SMEM)
        dma = pltpu.SemaphoreType.DMA
        zc, coef, halo, macro = pl.pallas_call(
            lambda *refs: moments_kernel(S, N, *refs),
            out_shape=(
                jax.ShapeDtypeStruct((nvx, 48, L), bf16),
                jax.ShapeDtypeStruct((ITERS + 1, nvx, L), f32),
                jax.ShapeDtypeStruct((group, 8, plane), f32),
                jax.ShapeDtypeStruct(macro_state.shape, f32),
            ),
            in_specs=[pl.BlockSpec(memory_space=pl.ANY), vmem, vmem, vmem, smem, vmem] + [vmem] * 5,
            out_specs=(vmem,) * 4,
            scratch_shapes=[
                pltpu.VMEM((V, L), bf16),
                pltpu.VMEM((NV1 * Q, L + TILE), f32),
                pltpu.VMEM((16, TILE), f32),
                pltpu.VMEM((N, 16, TILE), f32),
                pltpu.VMEM((16, TILE), f32),
                pltpu.VMEM((16, TILE), f32),
                pltpu.VMEM((8, TILE), f32),
                pltpu.VMEM((8, TILE), f32),
                pltpu.VMEM((N, 8, TILE), f32),
                pltpu.VMEM((N, 8, TILE), f32),
                pltpu.VMEM((group, 8, plane), f32),
                pltpu.VMEM((group, 8, plane), f32),
                pltpu.VMEM((ITERS, S, 8, TILE), f32),
                pltpu.VMEM((16, 16), f32),
                dma((nvx,)), dma((group, N)), dma((group, N)),
                dma((N,)), dma((N,)), dma((N,)), dma(()), dma((N,)), dma(()),
                dma((N,)), dma((N,)), dma((N,)), dma((N,)),
                dma((group,)), dma((group,)), dma((ITERS, S)), dma((ITERS, S)),
            ],
            compiler_params=pltpu.CompilerParams(
                collective_id=0, has_side_effects=True, vmem_limit_bytes=40 * 1024 * 1024),
        )(
            velocity_dist, macro_state, collision_rate[None, :], wall_flags[None, :], diffusivity, coupling,
            *(jnp.asarray(table[name]) for name in ("reduce", "project", "beta", "moments", "inner")),
        )
        dist = pl.pallas_call(
            lambda *refs: result_kernel(N, members, *refs),
            grid=(nvx,),
            out_shape=jax.ShapeDtypeStruct((V, L), bf16),
            in_specs=[
                pl.BlockSpec((plane, L), lambda j: (j, 0)),
                pl.BlockSpec((1, 48, L), lambda j: (j, 0, 0)),
                vmem, vmem, vmem,
            ],
            out_specs=pl.BlockSpec((plane, L), lambda j: (j, 0)),
            compiler_params=pltpu.CompilerParams(vmem_limit_bytes=40 * 1024 * 1024),
        )(velocity_dist, zc, coef, halo, jnp.asarray(table["phi"]))
        return dist, macro

    placed = (P("vel", "space"), P(None, ("space", "vel")), P("space"), P("space"), P(), P())
    return jax.shard_map(
        per_device,
        mesh=mesh,
        in_specs=placed,
        out_specs=(P("vel", "space"), P(None, ("space", "vel"))),
        check_vma=False,
    )
```

profile of v0, /device:TPU:0, one launch (start us, length us, event | category | flops | bytes accessed | tf_op | source)
XLA Modules:
  0.0 46.1 jit_solution(10192962604062970052)
XLA Ops:
  0.6 0.0 copy-start
  0.6 2.2 %copy-done = bf16[8192,256]{1,0:T(8,128)(2,1)S(1)} copy-done((bf16[8192,256]{1,0:T(8,128)(2,1)S(1)}, bf16[8192,256]{1,0:T(8,128)(2,1)}, u32[]{:S(2)}) %copy-start) | copy-done | bytes 4194328
  2.8 0.0 copy-start.2
  2.8 0.8 %copy-done.2 = bf16[256,48]{1,0:T(8,128)(2,1)S(1)} copy-done((bf16[256,48]{1,0:T(8,128)(2,1)S(1)}, bf16[256,48]{1,0:T(8,128)(2,1)}, u32[]{:S(2)}) %copy-start.2) | copy-done | bytes 24600
  3.7 0.0 copy-start.3
  3.7 0.8 %copy-done.3 = bf16[256,48]{1,0:T(8,128)(2,1)S(1)} copy-done((bf16[256,48]{1,0:T(8,128)(2,1)S(1)}, bf16[256,48]{1,0:T(8,128)(2,1)}, u32[]{:S(2)}) %copy-start.3) | copy-done | bytes 24600
  4.5 0.0 copy-start.4
  4.5 0.8 %copy-done.4 = bf16[16,1024]{1,0:T(8,128)(2,1)S(1)} copy-done((bf16[16,1024]{1,0:T(8,128)(2,1)S(1)}, bf16[16,1024]{1,0:T(8,128)(2,1)}, u32[]{:S(2)}) %copy-start.4) | copy-done | bytes 32792
  5.3 0.0 copy-start.5
  5.3 0.7 %copy-done.5 = bf16[32,256]{1,0:T(8,128)(2,1)S(1)} copy-done((bf16[32,256]{1,0:T(8,128)(2,1)S(1)}, bf16[32,256]{1,0:T(8,128)(2,1)}, u32[]{:S(2)}) %copy-start.5) | copy-done | bytes 16408
  6.0 0.0 copy-start.6
  6.0 0.7 %copy-done.6 = f32[13,64]{1,0:T(8,128)S(1)} copy-done((f32[13,64]{1,0:T(8,128)S(1)}, f32[13,64]{1,0:T(8,128)}, u32[]{:S(2)}) %copy-start.6) | copy-done | bytes 3352
  6.7 0.0 copy-start.7
  6.7 0.7 %copy-done.7 = f32[13,13]{1,0:T(8,128)S(1)} copy-done((f32[13,13]{1,0:T(8,128)S(1)}, f32[13,13]{1,0:T(8,128)}, u32[]{:S(2)}) %copy-start.7) | copy-done | bytes 700
  7.4 0.0 copy-start.8
  7.4 0.7 %copy-done.8 = bf16[16,48]{1,0:T(8,128)(2,1)S(1)} copy-done((bf16[16,48]{1,0:T(8,128)(2,1)S(1)}, bf16[16,48]{1,0:T(8,128)(2,1)}, u32[]{:S(2)}) %copy-start.8) | copy-done | bytes 1560
  8.1 0.0 copy-start.9
  8.1 0.7 %copy-done.9 = f32[256]{0:T(256)S(1)} copy-done((f32[256]{0:T(256)S(1)}, f32[256]{0:T(256)}, u32[]{:S(2)}) %copy-start.9) | copy-done | bytes 1048
  8.7 0.0 copy-start.10
  8.7 0.7 %copy-done.10 = s32[256]{0:T(256)S(1)} copy-done((s32[256]{0:T(256)S(1)}, s32[256]{0:T(256)}, u32[]{:S(2)}) %copy-start.10) | copy-done | bytes 1048
  9.4 0.0 copy-start.11
  9.4 0.7 %copy-done.11 = f32[13]{0:T(128)S(1)} copy-done((f32[13]{0:T(128)S(1)}, f32[13]{0:T(128)}, u32[]{:S(2)}) %copy-start.11) | copy-done | bytes 76
  10.1 0.0 copy-start.1
  10.1 28.8 %shard_map.131 = (bf16[8,48,256]{2,1,0:T(8,128)(2,1)S(1)}, f32[4,8,256]{2,1,0:T(8,128)S(1)}, f32[4,8,1024]{2,1,0:T(8,128)S(1)}, f32[13,64]{1,0:T(8,128)S(1)}) custom-call(bf16[8192,256]{1,0:T(8,128)(2,1)S(1)} %copy-done, f32[13,64]{1,0:T(8,128)S(1)} %copy-done.6, f32[1,256]{1,0:T(1,128)S(1)} %bitcast.2, s32[1,256]{1,0:T(1,128)S(1)} %bitcast.3, ...), custom_call_target="tpu_custom_call" | custom-call | tf_op jit(solution)/shard_map/pallas_call | solution.py:502
  38.8 0.0 copy-done.1
  38.9 6.6 %shard_map.132 = bf16[8192,256]{1,0:T(8,128)(2,1)} custom-call(bf16[8192,256]{1,0:T(8,128)(2,1)S(1)} %copy-done, bf16[8,48,256]{2,1,0:T(8,128)(2,1)S(1)} %get-tuple-element.6.refs_1_, f32[4,8,256]{2,1,0:T(8,128)S(1)} %get-tuple-element.7.refs_2_, f32[4,8,1024]{2,1,0:T(8,128)S(1)} %get-tuple-element.8.refs_3_, bf16[32,1024]{1,0:T(8,128)(2,1)S(1)} %copy-done.1), custom_call_target="tpu_custom_call" | custom-call | tf_op jit(solution)/shard_map/pallas_call | solution.py:538
  45.5 0.6 %copy.15 = f32[13,64]{1,0:T(8,128)} copy(f32[13,64]{1,0:T(8,128)S(1)} %get-tuple-element.13) | data formatting | bytes 6656
Async XLA Ops:
  0.6 2.2 %copy-start = (bf16[8192,256]{1,0:T(8,128)(2,1)S(1)}, bf16[8192,256]{1,0:T(8,128)(2,1)}, u32[]{:S(2)}) copy-start(bf16[8192,256]{1,0:T(8,128)(2,1)} %refs_0_.3) | copy-start | bytes 12582916
  2.8 0.8 %copy-start.2 = (bf16[256,48]{1,0:T(8,128)(2,1)S(1)}, bf16[256,48]{1,0:T(8,128)(2,1)}, u32[]{:S(2)}) copy-start(bf16[256,48]{1,0:T(8,128)(2,1)} %constant.14.clone.refs_8_) | copy-start | bytes 73732
  3.7 0.8 %copy-start.3 = (bf16[256,48]{1,0:T(8,128)(2,1)S(1)}, bf16[256,48]{1,0:T(8,128)(2,1)}, u32[]{:S(2)}) copy-start(bf16[256,48]{1,0:T(8,128)(2,1)} %constant.13.clone.refs_7_) | copy-start | bytes 73732
  4.5 0.8 %copy-start.4 = (bf16[16,1024]{1,0:T(8,128)(2,1)S(1)}, bf16[16,1024]{1,0:T(8,128)(2,1)}, u32[]{:S(2)}) copy-start(bf16[16,1024]{1,0:T(8,128)(2,1)} %constant.12.clone.refs_6_) | copy-start | bytes 98308
  5.3 0.7 %copy-start.5 = (bf16[32,256]{1,0:T(8,128)(2,1)S(1)}, bf16[32,256]{1,0:T(8,128)(2,1)}, u32[]{:S(2)}) copy-start(bf16[32,256]{1,0:T(8,128)(2,1)} %constant.15.clone.refs_9_) | copy-start | bytes 49156
  6.0 0.7 %copy-start.6 = (f32[13,64]{1,0:T(8,128)S(1)}, f32[13,64]{1,0:T(8,128)}, u32[]{:S(2)}) copy-start(f32[13,64]{1,0:T(8,128)} %refs_1_.1) | copy-start | bytes 9988
  6.7 0.7 %copy-start.7 = (f32[13,13]{1,0:T(8,128)S(1)}, f32[13,13]{1,0:T(8,128)}, u32[]{:S(2)}) copy-start(f32[13,13]{1,0:T(8,128)} %refs_5_.1) | copy-start | bytes 2032
  7.4 0.7 %copy-start.8 = (bf16[16,48]{1,0:T(8,128)(2,1)S(1)}, bf16[16,48]{1,0:T(8,128)(2,1)}, u32[]{:S(2)}) copy-start(bf16[16,48]{1,0:T(8,128)(2,1)} %constant.16.clone.refs_10_) | copy-start | bytes 4612
  8.1 0.7 %copy-start.9 = (f32[256]{0:T(256)S(1)}, f32[256]{0:T(256)}, u32[]{:S(2)}) copy-start(f32[256]{0:T(256)} %param.14) | copy-start | bytes 3076
  8.7 0.7 %copy-start.10 = (s32[256]{0:T(256)S(1)}, s32[256]{0:T(256)}, u32[]{:S(2)}) copy-start(s32[256]{0:T(256)} %param.15) | copy-start | bytes 3076
  9.4 0.7 %copy-start.11 = (f32[13]{0:T(128)S(1)}, f32[13]{0:T(128)}, u32[]{:S(2)}) copy-start(f32[13]{0:T(128)} %refs_4_.2) | copy-start | bytes 160
  10.1 28.8 %copy-start.1 = (bf16[32,1024]{1,0:T(8,128)(2,1)S(1)}, bf16[32,1024]{1,0:T(8,128)(2,1)}, u32[]{:S(2)}) copy-start(bf16[32,1024]{1,0:T(8,128)(2,1)} %constant.17.clone.refs_4_) | copy-start | bytes 196612
where the time goes:
time: 46.6 us; the launch traced here: 46.1 us
  Pallas kernels  35.4 us (76%)
  local copies, waits for them, and re-layouts  10 us (21%)
  between operations  0.67 us (1%)
    pallas_call x1, Pallas kernels, per_device(): pl.pallas_call(lambda *refs: moments_kernel(S, N, *refs), out_shape=(jax....  28.8 us
    unnamed x25, local copies, waits for them, and re-layouts  10 us
    pallas_call x1, Pallas kernels, per_device(): pl.pallas_call(lambda *refs: result_kernel(N, members, *refs), grid=(nvx,...  6.6 us

commit v1 on v0

--- a/solution.py
+++ b/solution.py
@@ -15,6 +15,7 @@
 Q = 8
 HALO = 8
 TILE = 128
+GRANT = 60 * 1024 * 1024
 MESH = pl.DeviceIdType.MESH
 
 speed_limit = 4.0
@@ -56,6 +57,17 @@
     project = np.einsum("qr,vrk->vqk", gram, beta).reshape(rows, 16)
     moments = (w1[:, None, None] * beta).reshape(rows, 16).T
     inner = moments @ project
+    c = np.repeat(time_step * np.abs(v), Q)
+    half = rows // 2
+    step = np.concatenate(
+        [
+            (moments * (1.0 - c)) @ project,
+            (moments * c)[:, half:] @ project[half:],
+            (moments * c)[:, :half] @ project[:half],
+            inner,
+        ],
+        axis=1,
+    )
 
     def left(a):
         high, low = two_parts(a)
@@ -71,6 +83,7 @@
         beta=left(beta.reshape(rows, 16)),
         moments=np.concatenate([m_h, m_l]),
         inner=left(inner),
+        step=left(step),
     )
 
 
@@ -94,14 +107,20 @@
 
 def moments_kernel(
     S, N,
-    h_ref, macro_ref, rate_ref, wall_ref, diff_ref, coup_ref,
-    reduce_ref, project_ref, beta_ref, moments_ref, inner_ref,
-    zc_ref, coef_ref, halo_ref, out_ref,
-    h_buf, g_all, cur_stage, cur_peers, cur_left, cur_right,
-    pack_l, pack_r, from_left, from_right, edge_send, edge_recv, sums, coup_pad,
-    h_sem, g_ssem, g_rsem, c_ssem, c_rsem, cl_ssem, cl_rsem, cr_ssem, cr_rsem,
+    h_ref, *refs,
+):
+    count = 11
+    sources = refs[:count]
+    band_hbm, zc_ref, halo_ref, out_ref = refs[count:count + 4]
+    buffers = refs[count + 4:2 * count + 4]
+    (
+    h_buf, band_ref, g_all, cur_stage, cur_peers, cur_left, cur_right,
+    pack_l, pack_r, from_left, from_right, edge_send, edge_recv, sums, coup_pad, diag_pad,
+    small_sem, band_sem, h_sem, g_ssem, g_rsem, c_ssem, c_rsem, cl_ssem, cl_rsem, cr_ssem, cr_rsem,
     pl_ssem, pl_rsem, pr_ssem, pr_rsem, e_ssem, e_rsem, s_ssem, s_rsem,
-):
+    ) = refs[2 * count + 4:]
+    (macro_ref, rate_ref, wall_ref, reduce_ref, diff_ref, coup_ref,
+     project_ref, beta_ref, moments_ref, inner_ref, step_ref) = buffers
     L = h_ref.shape[1]
     W = L + TILE
     width = macro_ref.shape[1]
@@ -118,8 +137,16 @@
     has_right = s < S - 1
     f32 = jnp.float32
 
+    def small(i):
+        return pltpu.make_async_copy(sources[i], buffers[i], small_sem.at[i])
+
+    for i in range(4):
+        small(i).start()
     for j in range(nvx):
         pltpu.make_async_copy(h_ref.at[pl.ds(j * plane, plane)], h_buf.at[pl.ds(j * plane, plane)], h_sem.at[j]).start()
+
+    for i in range(4, count):
+        small(i).start()
 
     cur_left[...] = jnp.zeros_like(cur_left)
     cur_right[...] = jnp.zeros_like(cur_right)
@@ -152,6 +179,9 @@
 
     beside = has_left.astype(jnp.int32) + has_right.astype(jnp.int32)
     greetings = (N - 1) + N * beside + (S - 1 - beside)
+
+    for i in range(4):
+        small(i).wait()
 
     relax = time_step * rate_ref[...] * (1.0 + wall_ref[...].astype(f32))
     edge_relax = jnp.where(p == 0, relax[:, :TILE], relax[:, L - TILE:])
@@ -159,16 +189,19 @@
     cur_stage[0:K, :] = jnp.concatenate([macro_ref[...]] * per_tile, axis=1)
     cur_stage[K:K + 1, :] = edge_relax
     cur_peers[p] = cur_stage[...]
+
     coup_pad[...] = jnp.zeros_like(coup_pad)
-    coup_pad[0:K, 0:K] = coup_ref[...]
+    diag_pad[...] = jnp.zeros_like(diag_pad)
 
     row8 = lax.broadcasted_iota(jnp.int32, (8, L), 0)
     col8 = lax.broadcasted_iota(jnp.int32, (8, L), 1)
-    upwind_cell = jnp.where(positive, L - 1 - col8, col8)
-    pick = []
-    for m in range(members):
-        t = row8 - 4 * m
-        pick.append(((t == upwind_cell) & (t >= 0) & (t < ITERS)).astype(f32).astype(jnp.bfloat16))
+    near = jnp.where(positive, col8, L - 1 - col8)
+    row_p = lax.broadcasted_iota(jnp.int32, (8, members * TILE), 0)
+    col_p = lax.broadcasted_iota(jnp.int32, (8, members * TILE), 1)
+    t_p = row_p % 4
+    picked = (row_p // 4 == col_p // TILE) & (t_p == jnp.where(positive, TILE - 1 - col_p % TILE, col_p % TILE))
+    pick = (picked & (t_p < ITERS)).astype(f32).astype(jnp.bfloat16)
+    edge_lanes = pl.ds(pl.multiple_of(jnp.where(positive, L - TILE, 0), TILE), TILE)
 
     reduce = reduce_ref[...]
     lane8 = lax.broadcasted_iota(jnp.int32, (8, TILE), 1)
@@ -197,7 +230,6 @@
     has_up = jnp.where(positive, s - 1, S - 2 - s) >= 0
 
     for g in range(group):
-        edge = jnp.zeros((8, plane), f32)
         for m in range(members):
             j = g * members + m
             pltpu.make_async_copy(
@@ -206,11 +238,9 @@
             both = dot(reduce, block)
             value = both[:Q] + both[Q:]
             g_all[pl.ds(pl.multiple_of(p * R + j * Q, 8), Q), 0:L] = value
-            edge = edge + lax.dot_general(pick[m], block, (((1,), (1,)), ((), ())), preferred_element_type=f32)
             here = (lane8 >= HALO * j) & (lane8 < HALO * (j + 1))
             packed_l = jnp.where(here, roll(value[:, :TILE], HALO * j), packed_l)
             packed_r = jnp.where(here, roll(value[:, L - TILE:], HALO * j - (TILE - HALO)), packed_r)
-        edge_send[g] = edge
         if g == 0:
             pl.semaphore_wait(barrier, greetings)
             for k in range(1, N):
@@ -229,27 +259,38 @@
         for k in range(1, N):
             g_copy(g, k).start()
 
+    pack_l[...] = packed_l
+    pack_r[...] = packed_r
+
+    def pack_copy(src, dst, ssem, rsem, device):
+        return pltpu.make_async_remote_copy(
+            src_ref=src, dst_ref=dst.at[p], send_sem=ssem, recv_sem=rsem.at[p], device_id=device, device_id_type=MESH)
+
+    @pl.when(has_left)
+    def _():
+        for q in range(N):
+            pack_copy(pack_l, from_right, pl_ssem.at[q], pl_rsem, (s - 1, q)).start()
+
+    @pl.when(has_right)
+    def _():
+        for q in range(N):
+            pack_copy(pack_r, from_left, pr_ssem.at[q], pr_rsem, (s + 1, q)).start()
+
+    for g in range(group):
+        block = jnp.concatenate(
+            [h_buf[j * plane:(j + 1) * plane, edge_lanes] for j in range(g * members, (g + 1) * members)], axis=1)
+        edge_send[g] = lax.dot_general(pick, block, (((1,), (1,)), ((), ())), preferred_element_type=f32)
+
         @pl.when(has_down)
         def _():
             edge_copy(g, downwind).start()
 
-    pack_l[...] = packed_l
-    pack_r[...] = packed_r
-
-    def pack_copy(src, dst, ssem, rsem, device):
-        return pltpu.make_async_remote_copy(
-            src_ref=src, dst_ref=dst.at[p], send_sem=ssem, recv_sem=rsem.at[p], device_id=device, device_id_type=MESH)
-
-    @pl.when(has_left)
-    def _():
-        for q in range(N):
-            pack_copy(pack_l, from_right, pl_ssem.at[q], pl_rsem, (s - 1, q)).start()
-
-    @pl.when(has_right)
-    def _():
-        for q in range(N):
-            pack_copy(pack_r, from_left, pr_ssem.at[q], pr_rsem, (s + 1, q)).start()
-
+    for i in range(4, count):
+        small(i).wait()
+    coup_pad[0:K, 0:K] = coup_ref[...]
+    eye = lax.broadcasted_iota(jnp.int32, (K, K), 0) == lax.broadcasted_iota(jnp.int32, (K, K), 1)
+    diag_pad[0:K, 0:K] = jnp.where(eye, jnp.broadcast_to(diff_ref[...], (K, K)), 0.0)
+    diffusion = jnp.sum(diag_pad[...], axis=1, keepdims=True)
     vx_row = lax.broadcasted_iota(jnp.int32, (NV1 * Q, 1), 0) // Q
     c_all = time_step * jnp.abs((vx_row.astype(f32) + 0.5) * (2.0 * speed_limit / NV1) - speed_limit)
     own_row = lax.broadcasted_iota(jnp.int32, (R, 1), 0) // Q + p * nvx
@@ -257,10 +298,8 @@
     own_vx = lax.broadcasted_iota(jnp.int32, (nvx, 1), 0) + p * nvx
     c_vx = time_step * jnp.abs((own_vx.astype(f32) + 0.5) * (2.0 * speed_limit / NV1) - speed_limit)
     row16 = lax.broadcasted_iota(jnp.int32, (16, 1), 0)
-    diffusion = jnp.zeros((16, 1), f32)
     scale = jnp.zeros((16, 1), f32)
     for k in range(K):
-        diffusion = jnp.where(row16 == k, diff_ref[k], diffusion)
         scale = jnp.where(row16 == k, shakhov_weights[k], scale)
     lane = lax.broadcasted_iota(jnp.int32, (1, W), 1)
     cell = jnp.where(lane < L + TILE // 2, lane, lane - W) + s * L
@@ -302,15 +341,22 @@
         shifted = [own_shift(a) for a in weights[:-1]]
         weights = [alpha * weights[0]] + [
             alpha * weights[i] + c_vx * shifted[i - 1] for i in range(1, ITERS + 1)]
-    for i in range(ITERS + 1):
-        coef_ref[i] = weights[i][:, :L]
-    for j in range(nvx):
-        m = j % members
-        t = row8 - 4 * m
+    def band_copy(j):
+        return pltpu.make_async_copy(band_ref.at[j], band_hbm.at[j], band_sem.at[j])
+
+    def bands(j):
+        row = lax.broadcasted_iota(jnp.int32, (L, L), 0)
+        col = lax.broadcasted_iota(jnp.int32, (L, L), 1)
+        distance = jnp.where(positive, col - row, row - col)
+        band = jnp.zeros((L, L), f32)
+        t = row8 - 4 * (j % members)
         value = jnp.zeros((8, L), f32)
-        for i in range(1, ITERS + 1):
-            near = jnp.where(positive, col8, L - 1 - col8)
-            value = jnp.where((near + 1 + t == i) & (t >= 0) & (t < ITERS), weights[i][j:j + 1, :L], value)
+        for i in range(ITERS + 1):
+            line = weights[i][j:j + 1, :L]
+            band = jnp.where(distance == i, line, band)
+            value = jnp.where((near + 1 + t == i) & (t >= 0) & (t < ITERS), line, value)
+        band_ref[j, 0:L, :], band_ref[j, L:2 * L, :] = split(band)
+        band_copy(j).start()
         high, low = split(value)
         zc_ref[j, 32:48, :] = jnp.concatenate([high.astype(f32), low.astype(f32)], axis=0).astype(jnp.bfloat16)
 
@@ -350,8 +396,9 @@
         return jnp.concatenate([roll(x[:half], -1), roll(x[half:], 1)], axis=0)
 
     def operator(r):
-        applied = jnp.dot(coupling, r, precision=lax.Precision.HIGHEST, preferred_element_type=f32)
-        applied = applied + diffusion * (2.0 * r - roll(r, 1) - roll(r, -1))
+        applied = diffusion * (2.0 * r - roll(r, 1) - roll(r, -1))
+        for k in range(K):
+            applied = applied + coupling[:, k:k + 1] * r[k:k + 1, :]
         return jnp.where(inside, applied, 0.0)
 
     def own_sum(x):
@@ -372,12 +419,24 @@
             src_ref=sums.at[n, s], dst_ref=sums.at[n, s], send_sem=s_ssem.at[n, t], recv_sem=s_rsem.at[n, s],
             device_id=(target, p), device_id_type=MESH)
 
+    def transport(x):
+        return keep_all * x + c_all * all_shift(x)
+
+    def moments_of(x):
+        high, low = split(x)
+        twice = dot(moments_ref[...], high)
+        return twice[:16] + twice[16:] + dot(moments_ref[0:16, :], low)
+
+    moved = transport(state)
+    base = moments_of(moved)
+    z = None
     for n in range(ITERS):
-        moved = keep_all * state + c_all * all_shift(state)
         pull = scale * relax * current
-        high, low = split(moved)
-        twice = dot(moments_ref[...], high)
-        shares = twice[:16] + twice[16:] + dot(moments_ref[0:16, :], low) + dot_parts(inner_ref[...], pull)
+        if n == 0:
+            shares = base + dot_parts(inner_ref[...], pull)
+        else:
+            shares = base + dot_parts(
+                step_ref[...], jnp.concatenate([z, roll(z, 1), roll(z, -1), pull - relax * z], axis=0))
         shares = jnp.where(inside, shares, 0.0)
         r = shares - current
         a1 = operator(r)
@@ -386,6 +445,16 @@
             [own_sum(r * r), own_sum(r * a1), own_sum(a1 * a1), own_sum(a1 * a2), jnp.zeros((4, TILE), f32)], axis=0)
         for t in range(1, S):
             sum_copy(n, t).start()
+        if n > 0:
+            fresh = dot_parts(beta_own, z)
+            source = fresh if source is None else drift + fresh
+            drift = keep_own * source + c_own * own_shift(source)
+        if n < ITERS - 1:
+            if n > 0:
+                moved = transport(moved + dot_parts(project_ref[...], z))
+            base = moments_of(transport(moved))
+        for j in range(n * nvx // ITERS, (n + 1) * nvx // ITERS):
+            bands(j)
         for t in range(1, S):
             q = lax.rem(s + t, S)
             pltpu.make_async_remote_copy(
@@ -401,10 +470,7 @@
         correction = first * r + second * (r - first * a1)
         current = shares + correction
         z = pull + correction
-        if n < ITERS - 1:
-            state = moved + dot_parts(project_ref[...], z)
-        fresh = dot_parts(beta_own, z)
-        source = fresh if source is None else keep_own * source + c_own * own_shift(source) + fresh
+    source = drift + dot_parts(beta_own, z)
 
     for j in range(nvx):
         high, low = split(source[j * Q:(j + 1) * Q, :L])
@@ -426,7 +492,11 @@
         for g in range(group):
             edge_copy(g, s).wait_recv()
 
-    halo_ref[...] = edge_recv[...]
+    for g in range(group):
+        halo_ref[g] = jnp.concatenate([edge_recv[g], edge_recv[g]], axis=0).astype(jnp.bfloat16)
+
+    for j in range(nvx):
+        band_copy(j).wait()
 
     for k in range(1, N):
         cur_copy(cur_peers.at[p], c_ssem.at[k], c_rsem.at[p], (s, lax.rem(p + k, N))).wait_send()
@@ -463,21 +533,17 @@
             sum_copy(n, t).wait_send()
 
 
-def result_kernel(N, members, h_ref, zc_ref, coef_ref, halo_ref, phi_ref, out_ref):
+def result_kernel(members, h_ref, band_ref, zc_ref, halo_ref, macro_ref, phi_ref, out_ref, macro_out_ref):
     j = pl.program_id(0)
     L = h_ref.shape[1]
-    positive = lax.axis_index("vel") >= N // 2
-    row = lax.broadcasted_iota(jnp.int32, (L, L), 0)
-    col = lax.broadcasted_iota(jnp.int32, (L, L), 1)
-    distance = jnp.where(positive, col - row, row - col)
-    band = jnp.zeros((L, L), jnp.float32)
-    for i in range(ITERS + 1):
-        band = jnp.where(distance == i, coef_ref[i, pl.ds(j, 1), :], band)
-    high, low = split(band)
+
+    @pl.when(j == 0)
+    def _():
+        macro_out_ref[...] = macro_ref[...]
+
     block = h_ref[...]
-    edge = halo_ref[j // members]
-    rows = jnp.concatenate([phi_ref[...], jnp.concatenate([edge, edge], axis=0).astype(jnp.bfloat16)], axis=0)
-    total = dot(block, high) + dot(block, low)
+    rows = jnp.concatenate([phi_ref[...], halo_ref[j // members]], axis=0)
+    total = dot(block, band_ref[0, 0:L, :]) + dot(block, band_ref[0, L:2 * L, :])
     total = total + lax.dot_general(
         rows, zc_ref[0], (((0,), (0,)), ((), ())), preferred_element_type=jnp.float32)
     out_ref[...] = total.astype(jnp.bfloat16)
@@ -497,20 +563,26 @@
         assert N % 2 == 0 and nvx % 2 == 0 and HALO * nvx <= TILE and width >= HALO and TILE % width == 0
         f32, bf16 = jnp.float32, jnp.bfloat16
         vmem = pl.BlockSpec(memory_space=pltpu.VMEM)
-        smem = pl.BlockSpec(memory_space=pltpu.SMEM)
+        hbm = pl.BlockSpec(memory_space=pltpu.HBM)
         dma = pltpu.SemaphoreType.DMA
-        zc, coef, halo, macro = pl.pallas_call(
+        small = [
+            macro_state, collision_rate[None, :], wall_flags[None, :], jnp.asarray(table["reduce"]),
+            diffusivity[None, :], coupling,
+        ] + [jnp.asarray(table[name]) for name in ("project", "beta", "moments", "inner", "step")]
+        band, zc, halo, macro = pl.pallas_call(
             lambda *refs: moments_kernel(S, N, *refs),
             out_shape=(
+                jax.ShapeDtypeStruct((nvx, 2 * L, L), bf16),
                 jax.ShapeDtypeStruct((nvx, 48, L), bf16),
-                jax.ShapeDtypeStruct((ITERS + 1, nvx, L), f32),
-                jax.ShapeDtypeStruct((group, 8, plane), f32),
+                jax.ShapeDtypeStruct((group, 16, plane), bf16),
                 jax.ShapeDtypeStruct(macro_state.shape, f32),
             ),
-            in_specs=[pl.BlockSpec(memory_space=pl.ANY), vmem, vmem, vmem, smem, vmem] + [vmem] * 5,
-            out_specs=(vmem,) * 4,
+            in_specs=[hbm] * (1 + len(small)),
+            out_specs=(hbm,) + (vmem,) * 3,
             scratch_shapes=[
+                *(pltpu.VMEM(x.shape, x.dtype) for x in small),
                 pltpu.VMEM((V, L), bf16),
+                pltpu.VMEM((nvx, 2 * L, L), bf16),
                 pltpu.VMEM((NV1 * Q, L + TILE), f32),
                 pltpu.VMEM((16, TILE), f32),
                 pltpu.VMEM((N, 16, TILE), f32),
@@ -524,30 +596,28 @@
                 pltpu.VMEM((group, 8, plane), f32),
                 pltpu.VMEM((ITERS, S, 8, TILE), f32),
                 pltpu.VMEM((16, 16), f32),
-                dma((nvx,)), dma((group, N)), dma((group, N)),
+                pltpu.VMEM((16, 16), f32),
+                dma((len(small),)), dma((nvx,)), dma((nvx,)), dma((group, N)), dma((group, N)),
                 dma((N,)), dma((N,)), dma((N,)), dma(()), dma((N,)), dma(()),
                 dma((N,)), dma((N,)), dma((N,)), dma((N,)),
                 dma((group,)), dma((group,)), dma((ITERS, S)), dma((ITERS, S)),
             ],
             compiler_params=pltpu.CompilerParams(
-                collective_id=0, has_side_effects=True, vmem_limit_bytes=40 * 1024 * 1024),
-        )(
-            velocity_dist, macro_state, collision_rate[None, :], wall_flags[None, :], diffusivity, coupling,
-            *(jnp.asarray(table[name]) for name in ("reduce", "project", "beta", "moments", "inner")),
-        )
-        dist = pl.pallas_call(
-            lambda *refs: result_kernel(N, members, *refs),
+                collective_id=0, has_side_effects=True, vmem_limit_bytes=GRANT),
+        )(velocity_dist, *small)
+        return pl.pallas_call(
+            lambda *refs: result_kernel(members, *refs),
             grid=(nvx,),
-            out_shape=jax.ShapeDtypeStruct((V, L), bf16),
+            out_shape=(jax.ShapeDtypeStruct((V, L), bf16), jax.ShapeDtypeStruct(macro_state.shape, f32)),
             in_specs=[
                 pl.BlockSpec((plane, L), lambda j: (j, 0)),
+                pl.BlockSpec((1, 2 * L, L), lambda j: (j, 0, 0)),
                 pl.BlockSpec((1, 48, L), lambda j: (j, 0, 0)),
                 vmem, vmem, vmem,
             ],
-            out_specs=pl.BlockSpec((plane, L), lambda j: (j, 0)),
-            compiler_params=pltpu.CompilerParams(vmem_limit_bytes=40 * 1024 * 1024),
-        )(velocity_dist, zc, coef, halo, jnp.asarray(table["phi"]))
-        return dist, macro
+            out_specs=(pl.BlockSpec((plane, L), lambda j: (j, 0)), vmem),
+            compiler_params=pltpu.CompilerParams(vmem_limit_bytes=GRANT),
+        )(velocity_dist, band, zc, halo, macro, jnp.asarray(table["phi"]))
 
     placed = (P("vel", "space"), P(None, ("space", "vel")), P("space"), P("space"), P(), P())
     return jax.shard_map(

time: 46.6 us -> 39.3 us (0.84)
  local copies, waits for them, and re-layouts: 10 us -> 0 us
  Pallas kernels: 35.4 us -> 38.4 us
    unnamed x25 -> x0, local copies, waits for them, and re-layouts: 10 us -> none
    pallas_call x1, Pallas kernels: 6.6 us -> 9.17 us  [per_device(): pl.pallas_call(lambda *refs: result_kernel(members, *refs), grid=(nvx,),...]
    pallas_call x1, Pallas kernels: 28.8 us -> 29.2 us  [per_device(): pl.pallas_call(lambda *refs: moments_kernel(S, N, *refs), out_shape=(jax....]
where the time goes in v1:
time: 39.3 us; the launch traced here: 39.1 us
  Pallas kernels  38.4 us (98%)
  between operations  0.64 us (2%)
    pallas_call x1, Pallas kernels, per_device(): pl.pallas_call(lambda *refs: moments_kernel(S, N, *refs), out_shape=(jax....  29.2 us
    pallas_call x1, Pallas kernels, per_device(): pl.pallas_call(lambda *refs: result_kernel(members, *refs), grid=(nvx,),...  9.17 us

profile of v1, /device:TPU:0, one launch (start us, length us, event | category | flops | bytes accessed | tf_op | source)
XLA Modules:
  0.0 39.1 jit_solution(16953466644040292841)
XLA Ops:
  0.6 29.2 %shard_map.140 = (bf16[8,512,256]{2,1,0:T(8,128)(2,1)}, bf16[8,48,256]{2,1,0:T(8,128)(2,1)}, bf16[4,16,1024]{2,1,0:T(8,128)(2,1)}, f32[13,64]{1,0:T(8,128)}) custom-call(bf16[8192,256]{1,0:T(8,128)(2,1)} %refs_0_.3, f32[13,64]{1,0:T(8,128)} %refs_1_.1, f32[1,256]{1,0:T(1,128)} %bitcast.3, s32[1,256]{1,0:T(1,128)} %bitcast.4, ...), custom_call_target="tpu_custom_call" | custom-call | tf_op jit(solution)/shard_map/pallas_call | solution.py:572
  29.9 9.2 %shard_map.141 = (bf16[8192,256]{1,0:T(8,128)(2,1)}, f32[13,64]{1,0:T(8,128)}) custom-call(bf16[8192,256]{1,0:T(8,128)(2,1)} %refs_0_.3, bf16[8,512,256]{2,1,0:T(8,128)(2,1)} %get-tuple-element.6.refs_1_, bf16[8,48,256]{2,1,0:T(8,128)(2,1)} %get-tuple-element.7.refs_2_, bf16[4,16,1024]{2,1,0:T(8,128)(2,1)} %get-tuple-element.8.refs_3_, ...), custom_call_target="tpu_custom_call" | custom-call | tf_op jit(solution)/shard_map/pallas_call | solution.py:608
